TPU v7x, 32 devices: a whole 2x2x4 slice. The times are simulated.
32 devices in a mesh: ma: 8 (over y, x, core), freq: 4 (over z).
Axes of the slice: x: 2, y: 2, z: 4, core: 2. Of those that a mesh axis runs over, the one named last changes fastest.
Arguments:
- visibilities: bfloat16 [2, 4096, 8, 1024], P(None, 'ma', 'freq'), may hold values from -0.099609375 to 0.099609375
- beam_modes: bfloat16 [32, 8, 2, 32, 1024], P('ma', 'freq'), may hold values from -0.125 to 0.125
- kl_vectors: bfloat16 [32, 2, 256, 256], P('ma', None, None, 'freq'), may hold values from -0.25 to 0.25
Outputs:
- kl_coeffs: float32 [32, 2, 256], P('ma', None, 'freq')
All inputs are finite; a program needn't handle non-finite values.
Results may differ from a plain program's by a relative error of at most 0.0046.
Values may be sent and summed in bfloat16 or wider, within the bound.
A program may use at most 64 MiB of HBM per device.

v0:
```python
import math

import jax
import jax.numpy as jnp
from jax import lax
from jax.sharding import PartitionSpec as P

NT = 4096


def phase_table(mode_count, first_time, time_count):
    mode_ids = jnp.arange(mode_count, dtype=jnp.int32)
    time_ids = first_time + jnp.arange(time_count, dtype=jnp.int32)
    phase_turns = mode_ids[:, None] * time_ids[None, :] % NT
    radians = phase_turns.astype(jnp.float32) * (2.0 * math.pi / NT)
    cosine = jnp.cos(radians)
    sine = jnp.sin(radians)
    twiddle = jnp.stack([jnp.stack([cosine, sine], 1), jnp.stack([-sine, cosine], 1)], 1)
    return twiddle.astype(jnp.bfloat16)


def shards(visibilities, beam_modes, kl_vectors):
    mode_rows = beam_modes.shape[0]
    fcount = visibilities.shape[2]
    base_count = visibilities.shape[3]
    time_rows = visibilities.shape[1]
    flat_rows = visibilities.reshape(2 * time_rows, fcount * base_count)
    first_time = lax.axis_index("ma") * time_rows
    twiddle = phase_table(mode_rows * lax.axis_size("ma"), first_time, time_rows)
    twiddle = twiddle.reshape(2 * (mode_rows * lax.axis_size("ma")), 2 * time_rows)
    summed = jnp.dot(twiddle, flat_rows, preferred_element_type=jnp.float32)
    by_mode = lax.psum_scatter(
        summed.reshape(mode_rows * lax.axis_size("ma"), 2, fcount, base_count),
        "ma",
        scatter_dimension=0,
        tiled=True,
    ).astype(jnp.bfloat16)
    products = jnp.einsum(
        "mfwsb,mcfb->wcmfs", beam_modes, by_mode, preferred_element_type=jnp.float32
    )
    real_part = products[0, 0] - products[1, 1]
    imag_part = products[1, 0] + products[0, 1]
    projected = jnp.stack([real_part, imag_part], 1).astype(jnp.bfloat16).reshape(mode_rows, 2, -1)
    coupled = jnp.einsum(
        "mwkx,mcx->wcmk", kl_vectors, projected, preferred_element_type=jnp.float32
    )
    partial_sums = jnp.stack([coupled[0, 0] - coupled[1, 1], coupled[0, 1] + coupled[1, 0]], 1)
    return lax.psum_scatter(partial_sums, "freq", scatter_dimension=2, tiled=True)


def solution(mesh):
    in_specs = (
        P(None, "ma", "freq", None),
        P("ma", "freq", None, None, None),
        P("ma", None, None, "freq"),
    )
    out_specs = P("ma", None, "freq")
    return jax.shard_map(shards, mesh=mesh, in_specs=in_specs, out_specs=out_specs, check_vma=False)
```

profile of v0, /device:TPU:0, one launch (start us, length us, event | category | flops | bytes accessed | tf_op | source)
XLA Modules:
  0.0 85.9 jit_solution(6234236856824570742)
XLA Ops:
  6.5 0.0 copy-start
  6.5 0.0 reduce-scatter.4.cloned.1.call-start
  6.5 5.6 %copy.39 = bf16[128,8,2,1024]{3,1,2,0:T(8,128)(2,1)} copy(bf16[128,8,2,1024]{3,2,1,0:T(2,128)(2,1)} %bitcast.49) | data formatting | bytes 8388608
  12.2 6.4 %copy.26 = bf16[2048,1024]{1,0:T(8,128)(2,1)} copy(bf16[2048,1024]{0,1:T(8,128)(2,1)} %bitcast.48) | data formatting | bytes 8388608 | tf_op jit(solution)/shard_map/dot_general | solution.py:31
  18.6 0.0 copy-start.2
  18.6 0.3 fusion.12
  18.9 0.0 copy-start.1
  18.9 0.1 copy.25
  19.0 0.1 copy.24
  19.1 3.6 %fusion = f32[32,2,2,1024]{3,0,2,1:T(8,128)S(1)} fusion(bf16[2,1024,1024,1]{2,1,0,3:T(8,128)(2,1)} %bitcast.47, bf16[32,1,1024]{2,0,1:T(8,128)(2,1)S(1)} %stack.34, bf16[32,1,1024]{2,0,1:T(8,128)(2,1)S(1)} %stack.32), kind=kOutput, calls=%fused_computation.3 | convolution fusion | flops 268697600 | bytes 4849664 | tf_op jit(solution)/shard_map/dot_general | solution.py:31
  22.7 0.4 copy.27
  23.1 31.9 %all-reduce.2 = bf16[32,2,2,1024]{3,1,2,0:T(2,128)(2,1)S(1)} all-reduce(f32[32,2,2,1024]{3,1,2,0:T(2,128)S(1)} %copy.27), channel_id=2, replica_groups=mesh['ma'=8,'freq'=4] {'ma'}, use_global_device_ids=true, to_apply=%region_0.1.clone | all-reduce | flops 131072 | bytes 786432
  55.1 0.0 copy-done.2
  55.1 0.6 dynamic-slice
  56.3 0.0 copy-done
  56.3 0.8 convolution_bitcast_fusion.1
  57.1 0.1 fusion.18
  57.1 0.1 add.69
  57.2 0.1 sub.31
  57.3 0.0 copy-done.1
  57.3 0.1 convolution_bitcast_fusion
  57.5 0.3 copy.35
  57.8 0.9 %reshape.222 = f32[256,8]{1,0:T(8,128)} reshape(f32[256,4,2]{2,1,0:T(4,128)S(1)} %bitcast.50) | data formatting | bytes 16384
  58.7 0.0 reduce-scatter.4.cloned.1.call-update
  58.7 18.7 %reduce-scatter.4.cloned.1.call-done = f32[64,8]{1,0:T(8,128)} async-done(((f32[256,8]{1,0:T(8,128)}), f32[64,8]{1,0:T(8,128)}) %reduce-scatter.4.cloned.1.call-update) | async-done | bytes 2064
  77.4 0.9 %reshape.223 = f32[64,4,2]{2,1,0:T(4,128)S(1)} reshape(f32[64,8]{1,0:T(8,128)} %reduce-scatter.4.cloned.1.call-done) | data formatting | bytes 4096
  78.3 0.7 copy.36
  (7 shorter events, 0.1 us)
Async XLA Ops:
  6.5 49.8 %copy-start = (bf16[4,2,2,32,1024]{4,3,2,1,0:T(8,128)(2,1)S(1)}, bf16[4,2,2,32,1024]{4,3,2,1,0:T(8,128)(2,1)}, u32[]{:S(2)}) copy-start(bf16[4,2,2,32,1024]{4,3,2,1,0:T(8,128)(2,1)} %param.4) | copy-start | bytes 3145732
  6.5 70.9 %reduce-scatter.4.cloned.1.call-start = ((), (), s32[]{:S(2)}) async-start(), calls=%async_computation.1 | async-start | bytes 163840
  18.6 36.5 %copy-start.2 = (u32[32]{0:T(128)S(1)}, u32[32]{0:T(128)}, u32[]{:S(2)}) copy-start(u32[32]{0:T(128)} %constant.30) | copy-start | bytes 388
  18.9 38.4 %copy-start.1 = (bf16[4,2,256,64]{2,3,1,0:T(8,128)(2,1)S(1)}, bf16[4,2,256,64]{2,3,1,0:T(8,128)(2,1)}, u32[]{:S(2)}) copy-start(bf16[4,2,256,64]{2,3,1,0:T(8,128)(2,1)} %param.5) | copy-start | bytes 786436
Sparse Core Ops, SparseCore 0:
  58.8 18.5 reduce-scatter.3
where the time goes:
time: 86.2 us; the launch traced here: 85.9 us
  blocking collectives  31.9 us (37%)
  waiting for transfers between devices  18.7 us (22%)
  local copies, waits for them, and re-layouts  16.1 us (19%)
  between operations  14.2 us (16%)
  matrix products  4.5 us (5%)
    unnamed x1, blocking collectives  31.9 us
    unnamed x2, waiting for transfers between devices  18.7 us
    unnamed x12, local copies, waits for them, and re-layouts  8.95 us
    dot_general x2, local copies, waits for them, and re-layouts, shards(): summed = jnp.dot(twiddle, flat_rows, preferred_element_type=jnp.float32)  6.81 us
    dot_general x1, matrix products, shards(): summed = jnp.dot(twiddle, flat_rows, preferred_element_type=jnp.float32)  3.58 us
  transfers between devices with their start and end apart: 1, of which 1 were waited for; matrix products, arithmetic and copies ran while one was open for 0% of the time, Pallas kernels for 0%

commit v1 on v0

v1 whole, which is shorter than its diff:
```python
import functools
import math

import jax
import jax.numpy as jnp
import numpy as np
from jax import lax
from jax.experimental import pallas as pl
from jax.experimental.pallas import tpu as pltpu
from jax.sharding import PartitionSpec as P

NT = 4096
LANES = 128
GROUP = 2
MESH = pl.DeviceIdType.MESH


def steps(count, body):
    if count <= 16:
        for i in range(count):
            body(i)
    else:
        lax.fori_loop(0, count, lambda i, c: (body(i), c)[1], 0)


def twiddle_rows(xp, first, time_count, modes, owners, fcount):
    m = xp.arange(owners * modes, dtype=xp.int32)
    t = first + xp.arange(time_count, dtype=xp.int32)
    turns = (m[:, None] * t[None, :]) % NT
    angle = turns.astype(xp.float32) * xp.float32(2.0 * math.pi / NT)
    cos, sin = xp.cos(angle), xp.sin(angle)
    table = xp.stack([xp.stack([cos, sin], 1), xp.stack([-sin, cos], 1)], 1)
    table = table.reshape(owners, modes, 2, 2, time_count).transpose(0, 2, 1, 3, 4)
    eye = xp.eye(fcount, dtype=xp.float32)
    full = table[:, :, :, None, :, :, None] * eye[:, None, None, :]
    return full.reshape(owners * 2 * modes * fcount, 2 * time_count * fcount)


def kernel(
    cfg, vis, table, beam, kl, out,
    vbuf, tw, bbuf, kbuf, total, send, recv, stage, zrecv,
    in_sem, ssem, rsem, zs_sem, zr_sem,
):
    n, nf, modes, fcount, kd, ntiles, table_whole = cfg
    groups = ntiles // GROUP
    wide = GROUP * LANES
    rows = 2 * modes * fcount
    half = modes * fcount
    me = lax.axis_index("ma")
    mine = lax.axis_index("freq")

    tw_copy = pltpu.make_async_copy(table.at[me] if table_whole else table, tw, in_sem.at[ntiles])
    tw_copy.start()
    vis_copies = []
    for b in range(ntiles):
        copy = pltpu.make_async_copy(
            vis.at[:, :, b * LANES:(b + 1) * LANES], vbuf.at[b], in_sem.at[b])
        copy.start()
        vis_copies.append(copy)
    late = []
    for w in range(2):
        late.append(pltpu.make_async_copy(beam.at[:, :, w], bbuf.at[w], in_sem.at[ntiles + 1 + w]))
        late.append(pltpu.make_async_copy(kl.at[:, w], kbuf.at[w], in_sem.at[ntiles + 3 + w]))
    for copy in late:
        copy.start()

    barrier = pltpu.get_barrier_semaphore()

    def greet_ma(o):
        pl.semaphore_signal(barrier, inc=1, device_id=(lax.rem(me + o + 1, n), mine), device_id_type=MESH)

    def greet_freq(o):
        pl.semaphore_signal(barrier, inc=1, device_id=(me, lax.rem(mine + o + 1, nf)), device_id_type=MESH)

    steps(n - 1, greet_ma)
    steps(nf - 1, greet_freq)

    def block_copy(g, o):
        peer = lax.rem(me + o + 1, n)
        return pltpu.make_async_remote_copy(
            src_ref=send.at[g, peer], dst_ref=recv.at[g, o],
            send_sem=ssem.at[g, o], recv_sem=rsem.at[g, o],
            device_id=(peer, mine), device_id_type=MESH)

    tw_copy.wait()
    for g in range(groups):
        pieces = []
        for b in range(g * GROUP, (g + 1) * GROUP):
            vis_copies[b].wait()
            pieces.append(vbuf.at[b].reshape(vbuf.shape[1] * fcount, LANES)[...])
        part = jnp.dot(tw[...], jnp.concatenate(pieces, 1), preferred_element_type=jnp.float32)
        total[g] = part.reshape(n, rows, wide)
        send[g] = part.reshape(n, rows, wide).astype(jnp.bfloat16)
        if g == 0:
            pl.semaphore_wait(barrier, n + nf - 2)
        steps(n - 1, lambda o: block_copy(g, o).start())

    for copy in late:
        copy.wait()
    acc = jnp.zeros((rows, half * bbuf.shape[3]), jnp.float32)
    for g in range(groups):
        steps(n - 1, lambda o: block_copy(g, o).wait_recv())
        spec = total[g, me]
        if n <= 16:
            for o in range(n - 1):
                spec = spec + recv[g, o].astype(jnp.float32)
        else:
            spec = lax.fori_loop(0, n - 1, lambda o, s: s + recv[g, o].astype(jnp.float32), spec)
        turned = jnp.concatenate([-spec[half:], spec[:half]], 0)
        for w, lhs in ((0, spec), (1, turned)):
            rhs = bbuf[w, :, :, :, g * wide:(g + 1) * wide].reshape(-1, wide)
            acc = acc + lax.dot_general(
                lhs.astype(jnp.bfloat16), rhs, (((1,), (1,)), ((), ())),
                preferred_element_type=jnp.float32)

    svd = bbuf.shape[3]
    cols = half * svd
    row = lax.broadcasted_iota(jnp.int32, (half, cols), 0)
    lane = lax.broadcasted_iota(jnp.int32, (half, cols), 1)
    own = row == lane // svd
    real = jnp.sum(jnp.where(own, acc[:half], 0.0), 0, keepdims=True)
    imag = jnp.sum(jnp.where(own, acc[half:], 0.0), 0, keepdims=True)
    row = lax.broadcasted_iota(jnp.int32, (2 * modes, cols), 0)
    lane = lax.broadcasted_iota(jnp.int32, (2 * modes, cols), 1)
    own = row // 2 == lane // (fcount * svd)
    first = row % 2 == 0
    straight = jnp.where(own, jnp.where(first, real, imag), 0.0).astype(jnp.bfloat16)
    crossed = jnp.where(own, jnp.where(first, -imag, real), 0.0).astype(jnp.bfloat16)
    coeffs = jnp.dot(straight, kbuf[0].reshape(cols, -1), preferred_element_type=jnp.float32)
    coeffs = coeffs + jnp.dot(crossed, kbuf[1].reshape(cols, -1), preferred_element_type=jnp.float32)
    for i in range(stage.shape[0]):
        stage[i] = coeffs[:, i * LANES:(i + 1) * LANES]

    share = LANES // kd

    def kl_copy(o):
        peer = lax.rem(mine + o + 1, nf)
        return pltpu.make_async_remote_copy(
            src_ref=stage.at[peer // share], dst_ref=zrecv.at[o],
            send_sem=zs_sem.at[o], recv_sem=zr_sem.at[o],
            device_id=(me, peer), device_id_type=MESH)

    steps(nf - 1, lambda o: kl_copy(o).start())
    mixed = stage[mine // share]
    steps(nf - 1, lambda o: kl_copy(o).wait_recv())
    for o in range(nf - 1):
        mixed = mixed + zrecv[o]
    result = mixed[:, :kd]
    for i in range(1, share):
        result = jnp.where(mine % share == i, mixed[:, i * kd:(i + 1) * kd], result)
    for m in range(modes):
        out[m] = result[2 * m:2 * m + 2]
    for g in range(groups):
        steps(n - 1, lambda o: block_copy(g, o).wait_send())
    steps(nf - 1, lambda o: kl_copy(o).wait_send())


def shards(visibilities, beam_modes, kl_vectors):
    n, nf = lax.axis_size("ma"), lax.axis_size("freq")
    parts, times, fcount, bases = visibilities.shape
    modes, _, _, svd, _ = beam_modes.shape
    klen, xs = kl_vectors.shape[2:]
    kd = klen // nf
    ntiles = bases // LANES
    groups, wide = ntiles // GROUP, GROUP * LANES
    rows = 2 * modes * fcount
    table_rows, table_cols = n * rows, parts * times * fcount
    table_whole = n * table_rows * table_cols <= 1 << 22
    if table_whole:
        table = jnp.asarray(np.stack([
            twiddle_rows(np, a * times, times, modes, n, fcount) for a in range(n)
        ]).astype(jnp.bfloat16))
    else:
        first = lax.axis_index("ma") * times
        table = twiddle_rows(jnp, first, times, modes, n, fcount).astype(jnp.bfloat16)
    cfg = (n, nf, modes, fcount, kd, ntiles, table_whole)
    f32, bf16 = jnp.float32, jnp.bfloat16
    dma = pltpu.SemaphoreType.DMA
    return pl.pallas_call(
        functools.partial(kernel, cfg),
        out_shape=jax.ShapeDtypeStruct((modes, 2, kd), f32),
        in_specs=[pl.BlockSpec(memory_space=pl.ANY)] * 4,
        out_specs=pl.BlockSpec(memory_space=pltpu.VMEM),
        scratch_shapes=[
            pltpu.VMEM((ntiles, parts * times, fcount, LANES), bf16),
            pltpu.VMEM((table_rows, table_cols), bf16),
            pltpu.VMEM((2, modes, fcount, svd, bases), bf16),
            pltpu.VMEM((2, modes, xs, klen), bf16),
            pltpu.VMEM((groups, n, rows, wide), f32),
            pltpu.VMEM((groups, n, rows, wide), bf16),
            pltpu.VMEM((groups, n - 1, rows, wide), bf16),
            pltpu.VMEM((klen // LANES, 2 * modes, LANES), f32),
            pltpu.VMEM((nf - 1, 2 * modes, LANES), f32),
            dma((ntiles + 5,)),
            dma((groups, n - 1)),
            dma((groups, n - 1)),
            dma((nf - 1,)),
            dma((nf - 1,)),
        ],
        compiler_params=pltpu.CompilerParams(
            collective_id=0, has_side_effects=True, vmem_limit_bytes=40 << 20),
    )(
        visibilities.reshape(parts * times, fcount, bases),
        table,
        beam_modes,
        kl_vectors.transpose(0, 1, 3, 2),
    )


def solution(mesh):
    in_specs = (
        P(None, "ma", "freq", None),
        P("ma", "freq", None, None, None),
        P("ma", None, None, "freq"),
    )
    out_specs = P("ma", None, "freq")
    return jax.shard_map(shards, mesh=mesh, in_specs=in_specs, out_specs=out_specs, check_vma=False)
```

time: 86.2 us -> 26.2 us (0.30)
  blocking collectives: 31.9 us -> 0 us
  Pallas kernels: 0 us -> 18.8 us
  waiting for transfers between devices: 18.7 us -> 0 us
  between operations: 14.2 us -> 0.01 us
  local copies, waits for them, and re-layouts: 16.1 us -> 7.14 us
  matrix products: 4.5 us -> 0 us
    unnamed x1 -> x0, blocking collectives: 31.9 us -> none
    pallas_call x0 -> x1, Pallas kernels: none -> 18.8 us  [shards(): pl.pallas_call(functools.partial(kernel, cfg), out_shape=jax.ShapeDtypeSt...]
    unnamed x2 -> x0, waiting for transfers between devices: 18.7 us -> none
    dot_general x2 -> x0, local copies, waits for them, and re-layouts: 6.81 us -> none  [shards(): summed = jnp.dot(twiddle, flat_rows, preferred_element_type=jnp.float32)]
    dot_general x3 -> x0, matrix products: 4.5 us -> none  [the longest x1 3.58 us: shards(): summed = jnp.dot(twiddle, flat_rows, preferred_element_type=jnp.float32)]
    unnamed x12 -> x9, local copies, waits for them, and re-layouts: 8.95 us -> 7.14 us
  transfers between devices with their start and end apart: 1 -> 0, of which waited for: 1 -> 0; matrix products, arithmetic and copies ran while one was open for 0% -> 0% of each run, Pallas kernels for 0% -> 0%
where the time goes in v1:
time: 26.2 us; the launch traced here: 25.9 us
  Pallas kernels  18.8 us (72%)
  local copies, waits for them, and re-layouts  7.14 us (27%)
    pallas_call x1, Pallas kernels, shards(): pl.pallas_call(functools.partial(kernel, cfg), out_shape=jax.ShapeDtypeSt...  18.8 us
    unnamed x9, local copies, waits for them, and re-layouts  7.14 us

profile of v1, /device:TPU:0, one launch (start us, length us, event | category | flops | bytes accessed | tf_op | source)
XLA Modules:
  0.0 25.9 jit_solution(400987795466849955)
XLA Ops:
  0.0 0.0 copy-start
  0.0 2.2 %copy-done = bf16[2,512,2,1024]{3,2,1,0:T(2,128)(2,1)S(1)} copy-done((bf16[2,512,2,1024]{3,2,1,0:T(2,128)(2,1)S(1)}, bf16[2,512,2,1024]{3,2,1,0:T(2,128)(2,1)}, u32[]{:S(2)}) %copy-start) | copy-done | bytes 4194328
  2.2 0.0 copy-start.1
  2.2 2.2 %copy-done.1 = bf16[8,128,2048]{2,1,0:T(8,128)(2,1)S(1)} copy-done((bf16[8,128,2048]{2,1,0:T(8,128)(2,1)S(1)}, bf16[8,128,2048]{2,1,0:T(8,128)(2,1)}, u32[]{:S(2)}) %copy-start.1) | copy-done | bytes 4194328
  4.4 0.0 copy-start.2
  4.4 1.2 %copy-done.2 = bf16[4,2,2,32,1024]{4,3,2,1,0:T(8,128)(2,1)S(1)} copy-done((bf16[4,2,2,32,1024]{4,3,2,1,0:T(8,128)(2,1)S(1)}, bf16[4,2,2,32,1024]{4,3,2,1,0:T(8,128)(2,1)}, u32[]{:S(2)}) %copy-start.2) | copy-done | bytes 1048600
  5.6 0.0 copy-start.3
  5.6 0.9 %copy-done.3 = bf16[4,2,256,64]{2,3,1,0:T(8,128)(2,1)S(1)} copy-done((bf16[4,2,256,64]{2,3,1,0:T(8,128)(2,1)S(1)}, bf16[4,2,256,64]{2,3,1,0:T(8,128)(2,1)}, u32[]{:S(2)}) %copy-start.3) | copy-done | bytes 262168
  6.6 18.8 %shard_map.46 = f32[4,2,64]{2,1,0:T(2,128)S(1)} custom-call(bf16[1024,2,1024]{2,1,0:T(2,128)(2,1)S(1)} %bitcast.2, bf16[8,128,2048]{2,1,0:T(8,128)(2,1)S(1)} %copy-done.1, bf16[4,2,2,32,1024]{4,3,2,1,0:T(8,128)(2,1)S(1)} %copy-done.2, bf16[4,2,64,256]{3,2,1,0:T(8,128)(2,1)S(1)} %bitcast.3), custom_call_target="tpu_custom_call" | custom-call | tf_op jit(solution)/shard_map/pallas_call | solution.py:179
  25.3 0.6 %copy.6 = f32[4,2,64]{2,1,0:T(2,128)} copy(f32[4,2,64]{2,1,0:T(2,128)S(1)} %shard_map.46) | data formatting | bytes 4096
Async XLA Ops:
  0.0 2.2 %copy-start = (bf16[2,512,2,1024]{3,2,1,0:T(2,128)(2,1)S(1)}, bf16[2,512,2,1024]{3,2,1,0:T(2,128)(2,1)}, u32[]{:S(2)}) copy-start(bf16[2,512,2,1024]{3,2,1,0:T(2,128)(2,1)} %param.4) | copy-start | bytes 12582916
  2.2 2.2 %copy-start.1 = (bf16[8,128,2048]{2,1,0:T(8,128)(2,1)S(1)}, bf16[8,128,2048]{2,1,0:T(8,128)(2,1)}, u32[]{:S(2)}) copy-start(bf16[8,128,2048]{2,1,0:T(8,128)(2,1)} %constant.2.clone.table) | copy-start | bytes 12582916
  4.4 1.2 %copy-start.2 = (bf16[4,2,2,32,1024]{4,3,2,1,0:T(8,128)(2,1)S(1)}, bf16[4,2,2,32,1024]{4,3,2,1,0:T(8,128)(2,1)}, u32[]{:S(2)}) copy-start(bf16[4,2,2,32,1024]{4,3,2,1,0:T(8,128)(2,1)} %beam.1) | copy-start | bytes 3145732
  5.6 0.9 %copy-start.3 = (bf16[4,2,256,64]{2,3,1,0:T(8,128)(2,1)S(1)}, bf16[4,2,256,64]{2,3,1,0:T(8,128)(2,1)}, u32[]{:S(2)}) copy-start(bf16[4,2,256,64]{2,3,1,0:T(8,128)(2,1)} %param.6) | copy-start | bytes 786436

commit v2 on v1

--- a/solution.py
+++ b/solution.py
@@ -198,7 +198,7 @@
             dma((nf - 1,)),
         ],
         compiler_params=pltpu.CompilerParams(
-            collective_id=0, has_side_effects=True, vmem_limit_bytes=40 << 20),
+            collective_id=0, has_side_effects=True, vmem_limit_bytes=60 << 20),
     )(
         visibilities.reshape(parts * times, fcount, bases),
         table,

time: 26.2 us -> 18.9 us (0.72)
  local copies, waits for them, and re-layouts: 7.14 us -> 1.28 us
  Pallas kernels: 18.8 us -> 17.4 us
    unnamed x9 -> x1, local copies, waits for them, and re-layouts: 7.14 us -> 1.28 us
    pallas_call x1, Pallas kernels: 18.8 us -> 17.4 us  [shards(): pl.pallas_call(functools.partial(kernel, cfg), out_shape=jax.ShapeDtypeSt...]
where the time goes in v2:
time: 18.9 us; the launch traced here: 18.7 us
  Pallas kernels  17.4 us (92%)
  local copies, waits for them, and re-layouts  1.28 us (7%)
    pallas_call x1, Pallas kernels, shards(): pl.pallas_call(functools.partial(kernel, cfg), out_shape=jax.ShapeDtypeSt...  17.4 us
    unnamed x1, local copies, waits for them, and re-layouts  1.28 us

profile of v2, /device:TPU:0, one launch (start us, length us, event | category | flops | bytes accessed | tf_op | source)
XLA Modules:
  0.0 18.7 jit_solution(12549473119071081517)
XLA Ops:
  0.0 17.4 %shard_map.46 = f32[4,2,64]{2,1,0:T(2,128)} custom-call(bf16[1024,2,1024]{2,1,0:T(2,128)(2,1)} %bitcast.2, bf16[8,128,2048]{2,1,0:T(8,128)(2,1)} %constant.2.clone.table, bf16[4,2,2,32,1024]{4,3,2,1,0:T(8,128)(2,1)} %beam.1, bf16[4,2,64,256]{3,2,1,0:T(8,128)(2,1)} %bitcast.3), custom_call_target="tpu_custom_call" | custom-call | tf_op jit(solution)/shard_map/pallas_call | solution.py:179
  17.4 1.3 %copy.6 = f32[4,2,64]{2,1,0:T(2,128)} copy(f32[4,2,64]{2,1,0:T(2,128)} %shard_map.46) | data formatting | bytes 4096

commit v3 on v2

--- a/solution.py
+++ b/solution.py
@@ -142,6 +142,9 @@
 
     steps(nf - 1, lambda o: kl_copy(o).start())
     mixed = stage[mine // share]
+    for g in range(groups):
+        steps(n - 1, lambda o: block_copy(g, o).wait_send())
+    steps(nf - 1, lambda o: kl_copy(o).wait_send())
     steps(nf - 1, lambda o: kl_copy(o).wait_recv())
     for o in range(nf - 1):
         mixed = mixed + zrecv[o]
@@ -150,9 +153,6 @@
         result = jnp.where(mine % share == i, mixed[:, i * kd:(i + 1) * kd], result)
     for m in range(modes):
         out[m] = result[2 * m:2 * m + 2]
-    for g in range(groups):
-        steps(n - 1, lambda o: block_copy(g, o).wait_send())
-    steps(nf - 1, lambda o: kl_copy(o).wait_send())
 
 
 def shards(visibilities, beam_modes, kl_vectors):

time: 18.9 us -> 18.8 us (level)
  no operation moved by 1% of the time
where the time goes in v3:
time: 18.8 us; the launch traced here: 18.6 us
  Pallas kernels  17.3 us (92%)
  local copies, waits for them, and re-layouts  1.28 us (7%)
    pallas_call x1, Pallas kernels, shards(): pl.pallas_call(functools.partial(kernel, cfg), out_shape=jax.ShapeDtypeSt...  17.3 us
    unnamed x1, local copies, waits for them, and re-layouts  1.28 us

profile of v3, /device:TPU:0, one launch (start us, length us, event | category | flops | bytes accessed | tf_op | source)
XLA Modules:
  0.0 18.6 jit_solution(14769080483374490485)
XLA Ops:
  0.0 17.3 %shard_map.46 = f32[4,2,64]{2,1,0:T(2,128)} custom-call(bf16[1024,2,1024]{2,1,0:T(2,128)(2,1)} %bitcast.2, bf16[8,128,2048]{2,1,0:T(8,128)(2,1)} %constant.2.clone.table, bf16[4,2,2,32,1024]{4,3,2,1,0:T(8,128)(2,1)} %beam.1, bf16[4,2,64,256]{3,2,1,0:T(8,128)(2,1)} %bitcast.3), custom_call_target="tpu_custom_call" | custom-call | tf_op jit(solution)/shard_map/pallas_call | solution.py:179
  17.4 1.3 %copy.6 = f32[4,2,64]{2,1,0:T(2,128)} copy(f32[4,2,64]{2,1,0:T(2,128)} %shard_map.46) | data formatting | bytes 4096

commit v4 on v3

--- a/solution.py
+++ b/solution.py
@@ -11,7 +11,7 @@
 
 NT = 4096
 LANES = 128
-GROUP = 2
+GROUP = 4
 MESH = pl.DeviceIdType.MESH
 
 

time: 18.8 us -> 19 us (1.011)
  Pallas kernels: 17.3 us -> 17.5 us
where the time goes in v4:
time: 19 us; the launch traced here: 18.8 us
  Pallas kernels  17.5 us (92%)
  local copies, waits for them, and re-layouts  1.28 us (7%)
    pallas_call x1, Pallas kernels, shards(): pl.pallas_call(functools.partial(kernel, cfg), out_shape=jax.ShapeDtypeSt...  17.5 us
    unnamed x1, local copies, waits for them, and re-layouts  1.28 us

profile of v4, /device:TPU:0, one launch (start us, length us, event | category | flops | bytes accessed | tf_op | source)
XLA Modules:
  0.0 18.8 jit_solution(13374279695232345457)
XLA Ops:
  0.0 17.5 %shard_map.46 = f32[4,2,64]{2,1,0:T(2,128)} custom-call(bf16[1024,2,1024]{2,1,0:T(2,128)(2,1)} %bitcast.2, bf16[8,128,2048]{2,1,0:T(8,128)(2,1)} %constant.2.clone.table, bf16[4,2,2,32,1024]{4,3,2,1,0:T(8,128)(2,1)} %beam.1, bf16[4,2,64,256]{3,2,1,0:T(8,128)(2,1)} %bitcast.3), custom_call_target="tpu_custom_call" | custom-call | tf_op jit(solution)/shard_map/pallas_call | solution.py:179
  17.5 1.3 %copy.6 = f32[4,2,64]{2,1,0:T(2,128)} copy(f32[4,2,64]{2,1,0:T(2,128)} %shard_map.46) | data formatting | bytes 4096
